TPU v7x, 32 devices: a whole 2x2x4 slice. The times are simulated.
32 devices in a mesh: path: 8 (over z, y), tile: 4 (over x, core).
Axes of the slice: x: 2, y: 2, z: 4, core: 2. Of those that a mesh axis runs over, the one named last changes fastest.
Arguments:
- state0: float32 [3, 8, 64, 4096], P(None, 'path', 'tile'), may hold values from -6 to 6
- intensity: float32 [8, 64, 4096], P('path', 'tile'), may hold values from -4 to 4
- absorption: float32 [64, 4096], P('tile', 'path'), may hold values from 0.5 to 2
- screen_adjoint: float32 [64, 4096], P('tile', 'path'), may hold values from -6 to 6
Outputs:
- state_adjoint: float32 [3, 8, 64, 4096], P(None, 'path', 'tile')
- absorption_grad: float32 [64, 4096], P('tile', 'path')
All inputs are finite; a program needn't handle non-finite values.
Results may differ from a plain program's by a relative error of at most 0.00002.
Values sent between devices are 32-bit elements; how exact they have to be, the bound alone decides.
A program may use at most 64 MiB of HBM per device.

v0:
```python
import jax
import jax.numpy as jnp
from jax import lax
from jax.sharding import PartitionSpec as P

STEPS = 8


KAPPA = 0.65
DAMPING = 0.99
HEATING = 0.06
COUPLING = 0.5


def padded(x, sides, width):
    for axis, dim in sides:
        size, length = (lax.axis_size(axis), x.shape[dim])
        up = [(i, (i + 1) % size) for i in range(size - 1)]
        down = [(j, i) for i, j in up]
        last = lax.slice_in_dim(x, length - width, length, axis=dim)
        initial = lax.slice_in_dim(x, 0, width, axis=dim)
        before = lax.ppermute(last, axis, up)
        after = lax.ppermute(initial, axis, down)
        x = jnp.concatenate([before, x, after], axis=dim)
    return x


def row_after(field):
    return jnp.pad(field[:, 1:, :], ((0, 0), (0, 1), (0, 0)))


def row_before(field):
    return jnp.pad(field[:, :-1, :], ((0, 0), (1, 0), (0, 0)))


def col_after(field):
    return jnp.pad(field[:, :, 1:], ((0, 0), (0, 0), (0, 1)))


def col_before(field):
    return jnp.pad(field[:, :, :-1], ((0, 0), (0, 0), (1, 0)))


def rows_inside(width, rows):
    first = lax.axis_index("tile") * rows - width
    where = first + jnp.arange(rows + 2 * width, dtype=jnp.int32)
    flags = (where >= 0) & (where < rows * lax.axis_size("tile"))
    return flags.astype(jnp.float32)[None, :, None]


def widen(field, width):
    return jnp.pad(field, ((0, 0), (width, width), (0, 0)))


def interior(field, width, rows):
    return field[:, width : width + rows, :]


def advance(density, across, along, heat, inside):
    across = (across - KAPPA * (row_after(density) - density)) * inside
    along = (along - KAPPA * (col_after(density) - density)) * inside
    density = (
        DAMPING * density
        - KAPPA * (across - row_before(across) + along - col_before(along))
        + HEATING * heat * (1.0 + COUPLING * density)
    ) * inside
    return (density, across, along)


def retreat(dual_density, dual_across, dual_along, heat, inside):
    dual_across = (dual_across - KAPPA * (dual_density - row_after(dual_density))) * inside
    dual_along = (dual_along - KAPPA * (dual_density - col_after(dual_density))) * inside
    dual_density = (
        (DAMPING + HEATING * COUPLING * heat) * dual_density
        + KAPPA * (dual_across - row_before(dual_across) + dual_along - col_before(dual_along))
    ) * inside
    return (dual_density, dual_across, dual_along)


def per_device(state0, intensity, absorption, screen_adjoint):
    absorb, screen = (
        lax.all_gather(absorption, "path", axis=1, tiled=True),
        lax.all_gather(screen_adjoint, "path", axis=1, tiled=True),
    )
    heating = absorb[None] * intensity
    rows = intensity.shape[1]
    start = (state0[0], state0[1], state0[2])
    blank = jnp.zeros_like(heating)
    dual_start = (screen[None], blank, blank, blank)
    inside = rows_inside(1, rows)
    heat_wide = widen(heating, 1)

    def forward_one(carry, unused):
        density, across, along = carry
        wide = padded(jnp.stack([density, across]), (("tile", 2),), 1)
        density, across, along = advance(wide[0], wide[1], widen(along, 1), heat_wide, inside)
        result = (interior(density, 1, rows), interior(across, 1, rows), interior(along, 1, rows))
        return (result, carry[0])

    final_state, history = lax.scan(forward_one, start, None, length=STEPS)

    def backward_one(carry, density_then):
        dual_density, dual_across, dual_along, grad_heat = carry
        grad_heat = grad_heat + HEATING * (1.0 + COUPLING * density_then) * dual_density
        wide = padded(jnp.stack([dual_density, dual_across]), (("tile", 2),), 1)
        dual_density, dual_across, dual_along = retreat(
            wide[0], wide[1], widen(dual_along, 1), heat_wide, inside
        )
        result = (
            interior(dual_density, 1, rows),
            interior(dual_across, 1, rows),
            interior(dual_along, 1, rows),
            grad_heat,
        )
        return (result, None)

    finals, unused = lax.scan(backward_one, dual_start, history, reverse=True)
    dual_density, dual_across, dual_along, grad_heat = finals
    state_adjoint = jnp.stack([dual_density, dual_across, dual_along])
    local_grad = jnp.sum(intensity * grad_heat, axis=0)
    absorption_grad = lax.psum_scatter(local_grad, "path", scatter_dimension=1, tiled=True)
    return (state_adjoint, absorption_grad)


def solution(mesh):
    return jax.shard_map(
        per_device,
        mesh=mesh,
        in_specs=(
            P(None, "path", "tile", None),
            P("path", "tile", None),
            P("tile", "path"),
            P("tile", "path"),
        ),
        out_specs=(P(None, "path", "tile", None), P("tile", "path")),
        check_vma=False,
    )
```

profile of v0, /device:TPU:1, one launch (start us, length us, event | category | flops | bytes accessed | tf_op | source)
XLA Modules:
  0.0 276.7 jit_solution(2223210218364528139)
XLA Ops:
  8.4 26.1 %all_gather.7 = f32[16,4096]{1,0:T(8,128)S(1)} all-gather(f32[16,512]{1,0:T(8,128)} %param.10), channel_id=1, replica_groups=mesh['path'=8,'tile'=4] {'path'}, dimensions={1}, use_global_device_ids=true | all-gather | bytes 294912 | tf_op jit(solution)/shard_map/all_gather | solution.py:82
  34.5 24.9 %all_gather.6 = f32[16,4096]{1,0:T(8,128)S(1)} all-gather(f32[16,512]{1,0:T(8,128)} %param.11), channel_id=1, replica_groups=mesh['path'=8,'tile'=4] {'path'}, dimensions={1}, use_global_device_ids=true | all-gather | bytes 294912 | tf_op jit(solution)/shard_map/all_gather | solution.py:83
  59.5 76.0 %while.40 = (s32[]{:T(128)}, f32[1,16,4096]{2,1,0:T(8,128)S(1)}, f32[1,16,4096]{2,1,0:T(8,128)S(1)}, f32[1,16,4096]{2,1,0:T(8,128)S(1)}, f32[8,1,16,4096]{3,2,1,...) while((s32[]{:T(128)}, f32[1,16,4096]{2,1,0:T(8,128)S(1)}, ...), condition=%wide.region_1.2_spmd.clone, body=%wide.region_0.1_spmd.clone.sunk | while | flops 1843292 | bytes 9568985 | solution.py:100
  59.5 14.7 %collective-permute-start = (f32[2,1,1,4096]{3,2,1,0:T(1,128)S(1)}, f32[2,1,1,4096]{3,2,1,0:T(1,128)S(1)}, u32[]{:S(2)}, u32[]{:S(2)}) collective-permute-start(f32[2,1,1,4096]{3,2,1,0:T(1,128)S(1)} %get-tuple-element.452), channel_id=1, source_target_pairs={{1,0},{2,1},{3,2},{5,4},{6,5},{7,6},{9,8},{10,9},{11,10},{13,12},{... | collective-permute-start | bytes 98312 | tf_op jit(solution)/shard_map/while/body/eval_jaxpr/ppermute | solution.py:23
  74.2 3.0 %collective-permute-start.1 = (f32[2,1,1,4096]{3,2,1,0:T(1,128)S(1)}, f32[2,1,1,4096]{3,2,1,0:T(1,128)S(1)}, u32[]{:S(2)}, u32[]{:S(2)}) collective-permute-start(f32[2,1,1,4096]{3,2,1,0:T(1,128)S(1)} %get-tuple-element.453), channel_id=1, source_target_pairs={{0,1},{1,2},{2,3},{4,5},{5,6},{6,7},{8,9},{9,10},{10,11},{12,13},{... | collective-permute-start | bytes 98312 | tf_op jit(solution)/shard_map/while/body/eval_jaxpr/ppermute | solution.py:22
  79.1 1.9 collective-permute-start
  81.1 4.2 %collective-permute-start.1 = (f32[2,1,1,4096]{3,2,1,0:T(1,128)S(1)}, f32[2,1,1,4096]{3,2,1,0:T(1,128)S(1)}, u32[]{:S(2)}, u32[]{:S(2)}) collective-permute-start(f32[2,1,1,4096]{3,2,1,0:T(1,128)S(1)} %get-tuple-element.453), channel_id=1, source_target_pairs={{0,1},{1,2},{2,3},{4,5},{5,6},{6,7},{8,9},{9,10},{10,11},{12,13},{... | collective-permute-start | bytes 98312 | tf_op jit(solution)/shard_map/while/body/eval_jaxpr/ppermute | solution.py:22
  87.2 1.9 collective-permute-start
  89.1 4.2 %collective-permute-start.1 = (f32[2,1,1,4096]{3,2,1,0:T(1,128)S(1)}, f32[2,1,1,4096]{3,2,1,0:T(1,128)S(1)}, u32[]{:S(2)}, u32[]{:S(2)}) collective-permute-start(f32[2,1,1,4096]{3,2,1,0:T(1,128)S(1)} %get-tuple-element.453), channel_id=1, source_target_pairs={{0,1},{1,2},{2,3},{4,5},{5,6},{6,7},{8,9},{9,10},{10,11},{12,13},{... | collective-permute-start | bytes 98312 | tf_op jit(solution)/shard_map/while/body/eval_jaxpr/ppermute | solution.py:22
  97.2 4.2 %collective-permute-start.1 = (f32[2,1,1,4096]{3,2,1,0:T(1,128)S(1)}, f32[2,1,1,4096]{3,2,1,0:T(1,128)S(1)}, u32[]{:S(2)}, u32[]{:S(2)}) collective-permute-start(f32[2,1,1,4096]{3,2,1,0:T(1,128)S(1)} %get-tuple-element.453), channel_id=1, source_target_pairs={{0,1},{1,2},{2,3},{4,5},{5,6},{6,7},{8,9},{9,10},{10,11},{12,13},{... | collective-permute-start | bytes 98312 | tf_op jit(solution)/shard_map/while/body/eval_jaxpr/ppermute | solution.py:22
  105.2 4.2 %collective-permute-start.1 = (f32[2,1,1,4096]{3,2,1,0:T(1,128)S(1)}, f32[2,1,1,4096]{3,2,1,0:T(1,128)S(1)}, u32[]{:S(2)}, u32[]{:S(2)}) collective-permute-start(f32[2,1,1,4096]{3,2,1,0:T(1,128)S(1)} %get-tuple-element.453), channel_id=1, source_target_pairs={{0,1},{1,2},{2,3},{4,5},{5,6},{6,7},{8,9},{9,10},{10,11},{12,13},{... | collective-permute-start | bytes 98312 | tf_op jit(solution)/shard_map/while/body/eval_jaxpr/ppermute | solution.py:22
  113.3 4.2 %collective-permute-start.1 = (f32[2,1,1,4096]{3,2,1,0:T(1,128)S(1)}, f32[2,1,1,4096]{3,2,1,0:T(1,128)S(1)}, u32[]{:S(2)}, u32[]{:S(2)}) collective-permute-start(f32[2,1,1,4096]{3,2,1,0:T(1,128)S(1)} %get-tuple-element.453), channel_id=1, source_target_pairs={{0,1},{1,2},{2,3},{4,5},{5,6},{6,7},{8,9},{9,10},{10,11},{12,13},{... | collective-permute-start | bytes 98312 | tf_op jit(solution)/shard_map/while/body/eval_jaxpr/ppermute | solution.py:22
  121.4 4.2 %collective-permute-start.1 = (f32[2,1,1,4096]{3,2,1,0:T(1,128)S(1)}, f32[2,1,1,4096]{3,2,1,0:T(1,128)S(1)}, u32[]{:S(2)}, u32[]{:S(2)}) collective-permute-start(f32[2,1,1,4096]{3,2,1,0:T(1,128)S(1)} %get-tuple-element.453), channel_id=1, source_target_pairs={{0,1},{1,2},{2,3},{4,5},{5,6},{6,7},{8,9},{9,10},{10,11},{12,13},{... | collective-permute-start | bytes 98312 | tf_op jit(solution)/shard_map/while/body/eval_jaxpr/ppermute | solution.py:22
  129.4 4.2 %collective-permute-start.1 = (f32[2,1,1,4096]{3,2,1,0:T(1,128)S(1)}, f32[2,1,1,4096]{3,2,1,0:T(1,128)S(1)}, u32[]{:S(2)}, u32[]{:S(2)}) collective-permute-start(f32[2,1,1,4096]{3,2,1,0:T(1,128)S(1)} %get-tuple-element.453), channel_id=1, source_target_pairs={{0,1},{1,2},{2,3},{4,5},{5,6},{6,7},{8,9},{9,10},{10,11},{12,13},{... | collective-permute-start | bytes 98312 | tf_op jit(solution)/shard_map/while/body/eval_jaxpr/ppermute | solution.py:22
  135.5 72.5 %while.41 = (s32[]{:T(128)}, f32[1,16,4096]{2,1,0:T(8,128)S(1)}, f32[1,16,4096]{2,1,0:T(8,128)S(1)}, f32[1,16,4096]{2,1,0:T(8,128)S(1)}, f32[1,16,4096]{2,1,0:T(...) while((s32[]{:T(128)}, f32[1,16,4096]{2,1,0:T(8,128)S(1)}, ...), condition=%wide.region_3.4_spmd.clone, body=%wide.region_2.3_spmd.clone.sunk | while | flops 2031710 | bytes 9240843 | solution.py:117
  137.5 4.2 %collective-permute-start.3 = (f32[2,1,1,4096]{3,2,1,0:T(1,128)S(1)}, f32[2,1,1,4096]{3,2,1,0:T(1,128)S(1)}, u32[]{:S(2)}, u32[]{:S(2)}) collective-permute-start(f32[2,1,1,4096]{3,2,1,0:T(1,128)S(1)} %get-tuple-element.467), channel_id=1, source_target_pairs={{0,1},{1,2},{2,3},{4,5},{5,6},{6,7},{8,9},{9,10},{10,11},{12,13},{... | collective-permute-start | bytes 98312 | tf_op jit(solution)/shard_map/while/body/eval_jaxpr/ppermute | solution.py:22
  146.6 4.2 %collective-permute-start.3 = (f32[2,1,1,4096]{3,2,1,0:T(1,128)S(1)}, f32[2,1,1,4096]{3,2,1,0:T(1,128)S(1)}, u32[]{:S(2)}, u32[]{:S(2)}) collective-permute-start(f32[2,1,1,4096]{3,2,1,0:T(1,128)S(1)} %get-tuple-element.467), channel_id=1, source_target_pairs={{0,1},{1,2},{2,3},{4,5},{5,6},{6,7},{8,9},{9,10},{10,11},{12,13},{... | collective-permute-start | bytes 98312 | tf_op jit(solution)/shard_map/while/body/eval_jaxpr/ppermute | solution.py:22
  155.7 4.2 %collective-permute-start.3 = (f32[2,1,1,4096]{3,2,1,0:T(1,128)S(1)}, f32[2,1,1,4096]{3,2,1,0:T(1,128)S(1)}, u32[]{:S(2)}, u32[]{:S(2)}) collective-permute-start(f32[2,1,1,4096]{3,2,1,0:T(1,128)S(1)} %get-tuple-element.467), channel_id=1, source_target_pairs={{0,1},{1,2},{2,3},{4,5},{5,6},{6,7},{8,9},{9,10},{10,11},{12,13},{... | collective-permute-start | bytes 98312 | tf_op jit(solution)/shard_map/while/body/eval_jaxpr/ppermute | solution.py:22
  164.7 4.2 %collective-permute-start.3 = (f32[2,1,1,4096]{3,2,1,0:T(1,128)S(1)}, f32[2,1,1,4096]{3,2,1,0:T(1,128)S(1)}, u32[]{:S(2)}, u32[]{:S(2)}) collective-permute-start(f32[2,1,1,4096]{3,2,1,0:T(1,128)S(1)} %get-tuple-element.467), channel_id=1, source_target_pairs={{0,1},{1,2},{2,3},{4,5},{5,6},{6,7},{8,9},{9,10},{10,11},{12,13},{... | collective-permute-start | bytes 98312 | tf_op jit(solution)/shard_map/while/body/eval_jaxpr/ppermute | solution.py:22
  173.8 4.2 %collective-permute-start.3 = (f32[2,1,1,4096]{3,2,1,0:T(1,128)S(1)}, f32[2,1,1,4096]{3,2,1,0:T(1,128)S(1)}, u32[]{:S(2)}, u32[]{:S(2)}) collective-permute-start(f32[2,1,1,4096]{3,2,1,0:T(1,128)S(1)} %get-tuple-element.467), channel_id=1, source_target_pairs={{0,1},{1,2},{2,3},{4,5},{5,6},{6,7},{8,9},{9,10},{10,11},{12,13},{... | collective-permute-start | bytes 98312 | tf_op jit(solution)/shard_map/while/body/eval_jaxpr/ppermute | solution.py:22
  182.8 4.2 %collective-permute-start.3 = (f32[2,1,1,4096]{3,2,1,0:T(1,128)S(1)}, f32[2,1,1,4096]{3,2,1,0:T(1,128)S(1)}, u32[]{:S(2)}, u32[]{:S(2)}) collective-permute-start(f32[2,1,1,4096]{3,2,1,0:T(1,128)S(1)} %get-tuple-element.467), channel_id=1, source_target_pairs={{0,1},{1,2},{2,3},{4,5},{5,6},{6,7},{8,9},{9,10},{10,11},{12,13},{... | collective-permute-start | bytes 98312 | tf_op jit(solution)/shard_map/while/body/eval_jaxpr/ppermute | solution.py:22
  191.9 4.2 %collective-permute-start.3 = (f32[2,1,1,4096]{3,2,1,0:T(1,128)S(1)}, f32[2,1,1,4096]{3,2,1,0:T(1,128)S(1)}, u32[]{:S(2)}, u32[]{:S(2)}) collective-permute-start(f32[2,1,1,4096]{3,2,1,0:T(1,128)S(1)} %get-tuple-element.467), channel_id=1, source_target_pairs={{0,1},{1,2},{2,3},{4,5},{5,6},{6,7},{8,9},{9,10},{10,11},{12,13},{... | collective-permute-start | bytes 98312 | tf_op jit(solution)/shard_map/while/body/eval_jaxpr/ppermute | solution.py:22
  200.9 4.2 %collective-permute-start.3 = (f32[2,1,1,4096]{3,2,1,0:T(1,128)S(1)}, f32[2,1,1,4096]{3,2,1,0:T(1,128)S(1)}, u32[]{:S(2)}, u32[]{:S(2)}) collective-permute-start(f32[2,1,1,4096]{3,2,1,0:T(1,128)S(1)} %get-tuple-element.467), channel_id=1, source_target_pairs={{0,1},{1,2},{2,3},{4,5},{5,6},{6,7},{8,9},{9,10},{10,11},{12,13},{... | collective-permute-start | bytes 98312 | tf_op jit(solution)/shard_map/while/body/eval_jaxpr/ppermute | solution.py:22
  209.7 60.1 %reduce-scatter.2.cloned.1.call-done = f32[16,512]{1,0:T(8,128)} async-done(((f32[16,4096]{1,0:T(8,128)}), f32[16,512]{1,0:T(8,128)}) %reduce-scatter.2.cloned.1.call-update) | async-done | bytes 32784 | tf_op jit(solution)/shard_map/reduce_scatter | solution.py:121
  (226 shorter events, 65.1 us)
Async XLA Ops:
  7.2 262.6 %reduce-scatter.2.cloned.1.call-start = ((), (), s32[]{:S(2)}) async-start(), calls=%async_computation.1 | async-start | bytes 294912 | tf_op jit(solution)/shard_map/reduce_scatter | solution.py:121
  59.5 18.5 %collective-permute-start = (f32[2,1,1,4096]{3,2,1,0:T(1,128)S(1)}, f32[2,1,1,4096]{3,2,1,0:T(1,128)S(1)}, u32[]{:S(2)}, u32[]{:S(2)}) collective-permute-start(f32[2,1,1,4096]{3,2,1,0:T(1,128)S(1)} %get-tuple-element.452), channel_id=1, source_target_pairs={{1,0},{2,1},{3,2},{5,4},{6,5},{7,6},{9,8},{10,9},{11,10},{13,12},{... | collective-permute-start | bytes 98312 | tf_op jit(solution)/shard_map/while/body/eval_jaxpr/ppermute | solution.py:23
  79.1 7.0 %collective-permute-start = (f32[2,1,1,4096]{3,2,1,0:T(1,128)S(1)}, f32[2,1,1,4096]{3,2,1,0:T(1,128)S(1)}, u32[]{:S(2)}, u32[]{:S(2)}) collective-permute-start(f32[2,1,1,4096]{3,2,1,0:T(1,128)S(1)} %get-tuple-element.452), channel_id=1, source_target_pairs={{1,0},{2,1},{3,2},{5,4},{6,5},{7,6},{9,8},{10,9},{11,10},{13,12},{... | collective-permute-start | bytes 98312 | tf_op jit(solution)/shard_map/while/body/eval_jaxpr/ppermute | solution.py:23
  81.1 5.2 %collective-permute-start.1 = (f32[2,1,1,4096]{3,2,1,0:T(1,128)S(1)}, f32[2,1,1,4096]{3,2,1,0:T(1,128)S(1)}, u32[]{:S(2)}, u32[]{:S(2)}) collective-permute-start(f32[2,1,1,4096]{3,2,1,0:T(1,128)S(1)} %get-tuple-element.453), channel_id=1, source_target_pairs={{0,1},{1,2},{2,3},{4,5},{5,6},{6,7},{8,9},{9,10},{10,11},{12,13},{... | collective-permute-start | bytes 98312 | tf_op jit(solution)/shard_map/while/body/eval_jaxpr/ppermute | solution.py:22
  87.2 7.0 %collective-permute-start = (f32[2,1,1,4096]{3,2,1,0:T(1,128)S(1)}, f32[2,1,1,4096]{3,2,1,0:T(1,128)S(1)}, u32[]{:S(2)}, u32[]{:S(2)}) collective-permute-start(f32[2,1,1,4096]{3,2,1,0:T(1,128)S(1)} %get-tuple-element.452), channel_id=1, source_target_pairs={{1,0},{2,1},{3,2},{5,4},{6,5},{7,6},{9,8},{10,9},{11,10},{13,12},{... | collective-permute-start | bytes 98312 | tf_op jit(solution)/shard_map/while/body/eval_jaxpr/ppermute | solution.py:23
  89.1 5.2 %collective-permute-start.1 = (f32[2,1,1,4096]{3,2,1,0:T(1,128)S(1)}, f32[2,1,1,4096]{3,2,1,0:T(1,128)S(1)}, u32[]{:S(2)}, u32[]{:S(2)}) collective-permute-start(f32[2,1,1,4096]{3,2,1,0:T(1,128)S(1)} %get-tuple-element.453), channel_id=1, source_target_pairs={{0,1},{1,2},{2,3},{4,5},{5,6},{6,7},{8,9},{9,10},{10,11},{12,13},{... | collective-permute-start | bytes 98312 | tf_op jit(solution)/shard_map/while/body/eval_jaxpr/ppermute | solution.py:22
  95.3 7.0 %collective-permute-start = (f32[2,1,1,4096]{3,2,1,0:T(1,128)S(1)}, f32[2,1,1,4096]{3,2,1,0:T(1,128)S(1)}, u32[]{:S(2)}, u32[]{:S(2)}) collective-permute-start(f32[2,1,1,4096]{3,2,1,0:T(1,128)S(1)} %get-tuple-element.452), channel_id=1, source_target_pairs={{1,0},{2,1},{3,2},{5,4},{6,5},{7,6},{9,8},{10,9},{11,10},{13,12},{... | collective-permute-start | bytes 98312 | tf_op jit(solution)/shard_map/while/body/eval_jaxpr/ppermute | solution.py:23
  97.2 5.2 %collective-permute-start.1 = (f32[2,1,1,4096]{3,2,1,0:T(1,128)S(1)}, f32[2,1,1,4096]{3,2,1,0:T(1,128)S(1)}, u32[]{:S(2)}, u32[]{:S(2)}) collective-permute-start(f32[2,1,1,4096]{3,2,1,0:T(1,128)S(1)} %get-tuple-element.453), channel_id=1, source_target_pairs={{0,1},{1,2},{2,3},{4,5},{5,6},{6,7},{8,9},{9,10},{10,11},{12,13},{... | collective-permute-start | bytes 98312 | tf_op jit(solution)/shard_map/while/body/eval_jaxpr/ppermute | solution.py:22
  103.3 7.0 %collective-permute-start = (f32[2,1,1,4096]{3,2,1,0:T(1,128)S(1)}, f32[2,1,1,4096]{3,2,1,0:T(1,128)S(1)}, u32[]{:S(2)}, u32[]{:S(2)}) collective-permute-start(f32[2,1,1,4096]{3,2,1,0:T(1,128)S(1)} %get-tuple-element.452), channel_id=1, source_target_pairs={{1,0},{2,1},{3,2},{5,4},{6,5},{7,6},{9,8},{10,9},{11,10},{13,12},{... | collective-permute-start | bytes 98312 | tf_op jit(solution)/shard_map/while/body/eval_jaxpr/ppermute | solution.py:23
  111.4 7.0 %collective-permute-start = (f32[2,1,1,4096]{3,2,1,0:T(1,128)S(1)}, f32[2,1,1,4096]{3,2,1,0:T(1,128)S(1)}, u32[]{:S(2)}, u32[]{:S(2)}) collective-permute-start(f32[2,1,1,4096]{3,2,1,0:T(1,128)S(1)} %get-tuple-element.452), channel_id=1, source_target_pairs={{1,0},{2,1},{3,2},{5,4},{6,5},{7,6},{9,8},{10,9},{11,10},{13,12},{... | collective-permute-start | bytes 98312 | tf_op jit(solution)/shard_map/while/body/eval_jaxpr/ppermute | solution.py:23
  119.4 7.0 %collective-permute-start = (f32[2,1,1,4096]{3,2,1,0:T(1,128)S(1)}, f32[2,1,1,4096]{3,2,1,0:T(1,128)S(1)}, u32[]{:S(2)}, u32[]{:S(2)}) collective-permute-start(f32[2,1,1,4096]{3,2,1,0:T(1,128)S(1)} %get-tuple-element.452), channel_id=1, source_target_pairs={{1,0},{2,1},{3,2},{5,4},{6,5},{7,6},{9,8},{10,9},{11,10},{13,12},{... | collective-permute-start | bytes 98312 | tf_op jit(solution)/shard_map/while/body/eval_jaxpr/ppermute | solution.py:23
  127.5 7.0 %collective-permute-start = (f32[2,1,1,4096]{3,2,1,0:T(1,128)S(1)}, f32[2,1,1,4096]{3,2,1,0:T(1,128)S(1)}, u32[]{:S(2)}, u32[]{:S(2)}) collective-permute-start(f32[2,1,1,4096]{3,2,1,0:T(1,128)S(1)} %get-tuple-element.452), channel_id=1, source_target_pairs={{1,0},{2,1},{3,2},{5,4},{6,5},{7,6},{9,8},{10,9},{11,10},{13,12},{... | collective-permute-start | bytes 98312 | tf_op jit(solution)/shard_map/while/body/eval_jaxpr/ppermute | solution.py:23
  135.6 6.3 %collective-permute-start.2 = (f32[2,1,1,4096]{3,2,1,0:T(1,128)S(1)}, f32[2,1,1,4096]{3,2,1,0:T(1,128)S(1)}, u32[]{:S(2)}, u32[]{:S(2)}) collective-permute-start(f32[2,1,1,4096]{3,2,1,0:T(1,128)S(1)} %get-tuple-element.466), channel_id=1, source_target_pairs={{1,0},{2,1},{3,2},{5,4},{6,5},{7,6},{9,8},{10,9},{11,10},{13,12},{... | collective-permute-start | bytes 98312 | tf_op jit(solution)/shard_map/while/body/eval_jaxpr/ppermute | solution.py:23
  137.5 5.2 %collective-permute-start.3 = (f32[2,1,1,4096]{3,2,1,0:T(1,128)S(1)}, f32[2,1,1,4096]{3,2,1,0:T(1,128)S(1)}, u32[]{:S(2)}, u32[]{:S(2)}) collective-permute-start(f32[2,1,1,4096]{3,2,1,0:T(1,128)S(1)} %get-tuple-element.467), channel_id=1, source_target_pairs={{0,1},{1,2},{2,3},{4,5},{5,6},{6,7},{8,9},{9,10},{10,11},{12,13},{... | collective-permute-start | bytes 98312 | tf_op jit(solution)/shard_map/while/body/eval_jaxpr/ppermute | solution.py:22
  144.7 6.3 %collective-permute-start.2 = (f32[2,1,1,4096]{3,2,1,0:T(1,128)S(1)}, f32[2,1,1,4096]{3,2,1,0:T(1,128)S(1)}, u32[]{:S(2)}, u32[]{:S(2)}) collective-permute-start(f32[2,1,1,4096]{3,2,1,0:T(1,128)S(1)} %get-tuple-element.466), channel_id=1, source_target_pairs={{1,0},{2,1},{3,2},{5,4},{6,5},{7,6},{9,8},{10,9},{11,10},{13,12},{... | collective-permute-start | bytes 98312 | tf_op jit(solution)/shard_map/while/body/eval_jaxpr/ppermute | solution.py:23
  153.7 6.3 %collective-permute-start.2 = (f32[2,1,1,4096]{3,2,1,0:T(1,128)S(1)}, f32[2,1,1,4096]{3,2,1,0:T(1,128)S(1)}, u32[]{:S(2)}, u32[]{:S(2)}) collective-permute-start(f32[2,1,1,4096]{3,2,1,0:T(1,128)S(1)} %get-tuple-element.466), channel_id=1, source_target_pairs={{1,0},{2,1},{3,2},{5,4},{6,5},{7,6},{9,8},{10,9},{11,10},{13,12},{... | collective-permute-start | bytes 98312 | tf_op jit(solution)/shard_map/while/body/eval_jaxpr/ppermute | solution.py:23
  162.8 6.3 %collective-permute-start.2 = (f32[2,1,1,4096]{3,2,1,0:T(1,128)S(1)}, f32[2,1,1,4096]{3,2,1,0:T(1,128)S(1)}, u32[]{:S(2)}, u32[]{:S(2)}) collective-permute-start(f32[2,1,1,4096]{3,2,1,0:T(1,128)S(1)} %get-tuple-element.466), channel_id=1, source_target_pairs={{1,0},{2,1},{3,2},{5,4},{6,5},{7,6},{9,8},{10,9},{11,10},{13,12},{... | collective-permute-start | bytes 98312 | tf_op jit(solution)/shard_map/while/body/eval_jaxpr/ppermute | solution.py:23
  164.7 5.2 %collective-permute-start.3 = (f32[2,1,1,4096]{3,2,1,0:T(1,128)S(1)}, f32[2,1,1,4096]{3,2,1,0:T(1,128)S(1)}, u32[]{:S(2)}, u32[]{:S(2)}) collective-permute-start(f32[2,1,1,4096]{3,2,1,0:T(1,128)S(1)} %get-tuple-element.467), channel_id=1, source_target_pairs={{0,1},{1,2},{2,3},{4,5},{5,6},{6,7},{8,9},{9,10},{10,11},{12,13},{... | collective-permute-start | bytes 98312 | tf_op jit(solution)/shard_map/while/body/eval_jaxpr/ppermute | solution.py:22
  171.8 6.3 %collective-permute-start.2 = (f32[2,1,1,4096]{3,2,1,0:T(1,128)S(1)}, f32[2,1,1,4096]{3,2,1,0:T(1,128)S(1)}, u32[]{:S(2)}, u32[]{:S(2)}) collective-permute-start(f32[2,1,1,4096]{3,2,1,0:T(1,128)S(1)} %get-tuple-element.466), channel_id=1, source_target_pairs={{1,0},{2,1},{3,2},{5,4},{6,5},{7,6},{9,8},{10,9},{11,10},{13,12},{... | collective-permute-start | bytes 98312 | tf_op jit(solution)/shard_map/while/body/eval_jaxpr/ppermute | solution.py:23
  173.8 5.2 %collective-permute-start.3 = (f32[2,1,1,4096]{3,2,1,0:T(1,128)S(1)}, f32[2,1,1,4096]{3,2,1,0:T(1,128)S(1)}, u32[]{:S(2)}, u32[]{:S(2)}) collective-permute-start(f32[2,1,1,4096]{3,2,1,0:T(1,128)S(1)} %get-tuple-element.467), channel_id=1, source_target_pairs={{0,1},{1,2},{2,3},{4,5},{5,6},{6,7},{8,9},{9,10},{10,11},{12,13},{... | collective-permute-start | bytes 98312 | tf_op jit(solution)/shard_map/while/body/eval_jaxpr/ppermute | solution.py:22
  180.9 6.3 %collective-permute-start.2 = (f32[2,1,1,4096]{3,2,1,0:T(1,128)S(1)}, f32[2,1,1,4096]{3,2,1,0:T(1,128)S(1)}, u32[]{:S(2)}, u32[]{:S(2)}) collective-permute-start(f32[2,1,1,4096]{3,2,1,0:T(1,128)S(1)} %get-tuple-element.466), channel_id=1, source_target_pairs={{1,0},{2,1},{3,2},{5,4},{6,5},{7,6},{9,8},{10,9},{11,10},{13,12},{... | collective-permute-start | bytes 98312 | tf_op jit(solution)/shard_map/while/body/eval_jaxpr/ppermute | solution.py:23
  190.0 6.3 %collective-permute-start.2 = (f32[2,1,1,4096]{3,2,1,0:T(1,128)S(1)}, f32[2,1,1,4096]{3,2,1,0:T(1,128)S(1)}, u32[]{:S(2)}, u32[]{:S(2)}) collective-permute-start(f32[2,1,1,4096]{3,2,1,0:T(1,128)S(1)} %get-tuple-element.466), channel_id=1, source_target_pairs={{1,0},{2,1},{3,2},{5,4},{6,5},{7,6},{9,8},{10,9},{11,10},{13,12},{... | collective-permute-start | bytes 98312 | tf_op jit(solution)/shard_map/while/body/eval_jaxpr/ppermute | solution.py:23
  199.0 6.3 %collective-permute-start.2 = (f32[2,1,1,4096]{3,2,1,0:T(1,128)S(1)}, f32[2,1,1,4096]{3,2,1,0:T(1,128)S(1)}, u32[]{:S(2)}, u32[]{:S(2)}) collective-permute-start(f32[2,1,1,4096]{3,2,1,0:T(1,128)S(1)} %get-tuple-element.466), channel_id=1, source_target_pairs={{1,0},{2,1},{3,2},{5,4},{6,5},{7,6},{9,8},{10,9},{11,10},{13,12},{... | collective-permute-start | bytes 98312 | tf_op jit(solution)/shard_map/while/body/eval_jaxpr/ppermute | solution.py:23
  200.9 5.2 %collective-permute-start.3 = (f32[2,1,1,4096]{3,2,1,0:T(1,128)S(1)}, f32[2,1,1,4096]{3,2,1,0:T(1,128)S(1)}, u32[]{:S(2)}, u32[]{:S(2)}) collective-permute-start(f32[2,1,1,4096]{3,2,1,0:T(1,128)S(1)} %get-tuple-element.467), channel_id=1, source_target_pairs={{0,1},{1,2},{2,3},{4,5},{5,6},{6,7},{8,9},{9,10},{10,11},{12,13},{... | collective-permute-start | bytes 98312 | tf_op jit(solution)/shard_map/while/body/eval_jaxpr/ppermute | solution.py:22
  (10 other events, 98.1 us)
Sparse Core Ops, SparseCore 0:
  208.9 60.8 reduce-scatter.1
where the time goes:
time: 280 us; the launch traced here: 277 us
  starting transfers between devices  110 us (39%)
  waiting for transfers between devices  68.9 us (25%)
  blocking collectives  51 us (18%)
  other arithmetic  19.4 us (7%)
  between operations  14.1 us (5%)
  local copies, waits for them, and re-layouts  12 us (4%)
    ppermute x16, starting transfers between devices, padded(): before = lax.ppermute(last, axis, up)  66.4 us
    reduce_scatter x1, waiting for transfers between devices, per_device(): lax.psum_scatter(local_grad, 'path', scatter_dimension=1, tiled=True)  60.1 us
    ppermute x16, starting transfers between devices, padded(): after = lax.ppermute(initial, axis, down)  43.5 us
    all_gather x1, blocking collectives, per_device(): lax.all_gather(absorption, 'path', axis=1, tiled=True)  26.1 us
    all_gather x1, blocking collectives, per_device(): lax.all_gather(screen_adjoint, 'path', axis=1, tiled=True)  24.9 us
    mul x8, other arithmetic, retreat(): ((DAMPING + HEATING * COUPLING * heat) * dual_density + KAPPA * (dual_acr...  10.4 us
    ppermute x16, waiting for transfers between devices, padded(): before = lax.ppermute(last, axis, up)  8.71 us
    dynamic_update_slice x8, local copies, waits for them, and re-layouts, per_device(): final_state, history = lax.scan(forward_one, start, None, length=STEPS)  5.9 us
  transfers between devices with their start and end apart: 33, of which 17 were waited for; matrix products, arithmetic and copies ran while one was open for 3% of the time, Pallas kernels for 0%

commit v1 on v0

v1 whole, which is shorter than its diff:
```python
import functools

import jax
import jax.numpy as jnp
from jax import lax
from jax.experimental import pallas as pl
from jax.experimental.pallas import tpu as pltpu
from jax.sharding import PartitionSpec as P

MESH = pl.DeviceIdType.MESH
STEPS = 8
KAPPA = 0.65
DAMPING = 0.99
HEATING = 0.06
COUPLING = 0.5
LANES = 128
SUB = 8
DEPTH = 4
TOP = 2 * SUB
GROUP = 4


def kernel(n, tiles, state, light, absorb, screen, out_state, out_grad,
           xb, yb, wy, maps, beam, ub, vb, stage, total, part, share, done, gsum,
           load_sem, ag_send, ag_recv, hx_send, hx_recv, hq_send, hq_recv, rs_send, rs_recv, out_sem):
    depth = DEPTH if n % DEPTH == 0 else 1
    wide = n // depth
    row_tiles, cols = light.shape[0], light.shape[1]
    rows = row_tiles * SUB
    span = rows + 2 * SUB
    block = cols // n
    me = lax.axis_index("path")
    tile = lax.axis_index("tile")
    my_z, my_y = me // wide, lax.rem(me, wide)
    has_up, has_down = tile > 0, tile < tiles - 1

    loads = []
    for i in range(row_tiles):
        low = pl.ds(i * SUB, SUB)
        own = pl.ds(me * block, block)
        for src, dst in (
            (absorb.at[i], maps.at[0, own, low]),
            (screen.at[i], maps.at[1, own, low]),
            (light.at[i], beam.at[:, low]),
            (state.at[1, i], ub.at[:, low]),
            (state.at[2, i], vb.at[pl.ds(1, cols), low]),
            (state.at[0, i], xb.at[1, pl.ds(1, cols), pl.ds(TOP + i * SUB, SUB)]),
        ):
            loads.append(pltpu.make_async_copy(src, dst, load_sem.at[len(loads)]))
            loads[-1].start()

    barrier = pltpu.get_barrier_semaphore()
    for d in range(1, n):
        pl.semaphore_signal(barrier, inc=1, device_id={"path": lax.rem(me + d, n)}, device_id_type=MESH)

    @pl.when(has_up)
    def _():
        pl.semaphore_signal(barrier, inc=1, device_id={"tile": tile - 1}, device_id_type=MESH)

    @pl.when(has_down)
    def _():
        pl.semaphore_signal(barrier, inc=1, device_id={"tile": tile + 1}, device_id_type=MESH)

    greeted = n - 1 + has_up.astype(jnp.int32) + has_down.astype(jnp.int32)
    pl.semaphore_wait(barrier, greeted)

    def map_copy(owner, target, slot):
        ref = maps.at[:, pl.ds(owner * block, block)]
        return pltpu.make_async_remote_copy(
            src_ref=ref, dst_ref=ref, send_sem=ag_send.at[slot], recv_sem=ag_recv.at[owner],
            device_id={"path": target}, device_id_type=MESH)

    for i in range(row_tiles):
        loads[6 * i].wait()
        loads[6 * i + 1].wait()
    sends = []
    for d in [x for x in (2, 1, 3) if x < depth]:
        sends.append(map_copy(me, lax.rem(my_z + d, depth) * wide + my_y, len(sends)))
        sends[-1].start()
    for d in range(1, wide):
        sends.append(map_copy(me, my_z * wide + lax.rem(my_y + d, wide), len(sends)))
        sends[-1].start()

    blank = jnp.zeros((span, LANES), jnp.float32)
    vb[0] = jnp.zeros((rows, LANES), jnp.float32)
    total[cols] = jnp.zeros((rows + SUB, LANES), jnp.float32)
    for t in range(1, STEPS + 1):
        xb[t, cols + 1, pl.ds(SUB, span)] = blank
        yb[t, cols + 1, pl.ds(SUB, span)] = blank

    @pl.loop(0, cols)
    def _(j):
        wy[j] = blank

    strip = jnp.zeros((2, SUB, LANES), jnp.float32)

    @pl.when(jnp.logical_not(has_up))
    def _():
        @pl.loop(0, cols)
        def _(j):
            xb[pl.ds(0, 2), 1 + j, pl.ds(SUB, SUB)] = strip
            yb[pl.ds(0, 2), 1 + j, pl.ds(SUB, SUB)] = strip

    @pl.when(jnp.logical_not(has_down))
    def _():
        @pl.loop(0, cols)
        def _(j):
            xb[pl.ds(0, 2), 1 + j, pl.ds(TOP + rows, SUB)] = strip
            yb[pl.ds(0, 2), 1 + j, pl.ds(TOP + rows, SUB)] = strip

    for i in range(row_tiles):
        for c in range(2, 6):
            loads[6 * i + c].wait()
    row_of = lax.broadcasted_iota(jnp.int32, (rows, LANES), 0)
    lane_of = lax.broadcasted_iota(jnp.int32, (rows, LANES), 1)

    @pl.loop(0, cols)
    def _(j):
        u, v = ub[j], vb[1 + j]
        before = jnp.where(row_of == 0, 0.0, pltpu.roll(u, 1, 0))
        left = jnp.where(lane_of == 0, pltpu.roll(vb[j], 1, 1), pltpu.roll(v, 1, 1))
        w = KAPPA * ((u - before) + (v - left))
        xb[0, 1 + j, pl.ds(TOP, rows)] = w
        density = xb[1, 1 + j, pl.ds(TOP, rows)]
        stage[0, 0, j] = w[:SUB]
        stage[0, 1, j] = density[:SUB]
        last = KAPPA * pltpu.roll(u[rows - SUB:], 1, 0)
        stage[1, 0, j] = jnp.where(row_of[:SUB] == 0, last, w[rows - SUB:])
        stage[1, 1, j] = density[rows - SUB:]

    def state_copy(way):
        return pltpu.make_async_remote_copy(
            src_ref=stage.at[way],
            dst_ref=xb.at[pl.ds(0, 2), pl.ds(1, cols), pl.ds(TOP + rows if way == 0 else SUB, SUB)],
            send_sem=hx_send.at[way], recv_sem=hx_recv.at[way],
            device_id={"tile": tile - 1 if way == 0 else tile + 1}, device_id_type=MESH)

    def heat_copy(way, owner):
        at = pl.ds(1 + owner * block, block)
        first = TOP if way == 0 else TOP + rows - SUB
        return pltpu.make_async_remote_copy(
            src_ref=yb.at[pl.ds(0, 2), at, pl.ds(first, SUB)],
            dst_ref=yb.at[pl.ds(0, 2), at, pl.ds(TOP + rows if way == 0 else SUB, SUB)],
            send_sem=hq_send.at[way, owner], recv_sem=hq_recv.at[way, owner],
            device_id={"tile": tile - 1 if way == 0 else tile + 1}, device_id_type=MESH)

    @pl.when(has_up)
    def _():
        state_copy(0).start()

    @pl.when(has_down)
    def _():
        state_copy(1).start()

    def use(owner):
        for i in range(block):
            j = owner * block + i
            yb[0, 1 + j, pl.ds(TOP, rows)] = HEATING * (maps[0, j] * beam[j])
            yb[1, 1 + j, pl.ds(TOP, rows)] = maps[1, j]

        @pl.when(has_up)
        def _():
            heat_copy(0, owner).start()

        @pl.when(has_down)
        def _():
            heat_copy(1, owner).start()

    use(me)
    for d in [x for x in (1, 3, 2) if x < depth]:
        owner = lax.rem(my_z + d, depth) * wide + my_y
        map_copy(owner, owner, 0).wait_recv()
        for e in range(1, wide):
            sends.append(map_copy(owner, my_z * wide + lax.rem(my_y + e, wide), len(sends)))
            sends[-1].start()
        use(owner)
    for d in [x for x in (0, 1, 3, 2) if x < depth]:
        for e in range(1, wide):
            owner = lax.rem(my_z + d, depth) * wide + lax.rem(my_y + e, wide)
            map_copy(owner, owner, 0).wait_recv()
            use(owner)

    @pl.when(has_up)
    def _():
        state_copy(1).wait_recv()

        @pl.loop(0, cols)
        def _(j):
            above = jnp.where(row_of[:SUB] == 0, xb[0, 1 + j, pl.ds(SUB, SUB)], 0.0)
            xb[0, 1 + j, pl.ds(TOP, SUB)] = xb[0, 1 + j, pl.ds(TOP, SUB)] - above

    @pl.when(has_down)
    def _():
        state_copy(0).wait_recv()

        @pl.loop(0, cols)
        def _(j):
            last = KAPPA * pltpu.roll(ub[j, pl.ds(rows - SUB, SUB)], 1, 0)
            above = jnp.where(row_of[:SUB] == 0, last, 0.0)
            xb[0, 1 + j, pl.ds(TOP + rows, SUB)] = xb[0, 1 + j, pl.ds(TOP + rows, SUB)] - above

    @pl.when(has_up)
    def _():
        @pl.loop(0, n)
        def _(b):
            heat_copy(1, b).wait_recv()

    @pl.when(has_down)
    def _():
        @pl.loop(0, n)
        def _(b):
            heat_copy(0, b).wait_recv()

    place = tile * rows - SUB + lax.broadcasted_iota(jnp.int32, (span, LANES), 0)
    inside = (place >= 0) & (place < tiles * rows)
    near = jnp.where(inside, KAPPA * KAPPA, 0.0)
    here = jnp.where(place == 0, 3.0, 4.0) * (KAPPA * KAPPA)
    lane = lax.broadcasted_iota(jnp.int32, (span, LANES), 1)

    def pad_left(field, t):
        field[t, 0, pl.ds(SUB, span)] = pltpu.roll(field[t, 1, pl.ds(SUB, span)], LANES - 1, 1)

    pad_left(xb, 1)
    pad_left(yb, 1)

    def spread(field, t, first, count, start, size, near, here, lane):
        window = [field[t, first + i, pl.ds(start, size)] for i in range(count + 2)]
        right = [pltpu.roll(x, 1, 1) for x in window[:-1]]
        left = [pltpu.roll(x, LANES - 1, 1) for x in window[1:]]
        found = []
        for i in range(count):
            before = jnp.where(lane == 0, right[i], right[i + 1])
            after = jnp.where(lane == LANES - 1, left[i + 1], left[i])
            upper = field[t, first + 1 + i, pl.ds(start - 1, size)]
            lower = field[t, first + 1 + i, pl.ds(start + 1, size)]
            x = window[i + 1]
            found.append((x, near * ((before + after) + (upper + lower)) - here * x))
        return found

    @pl.loop(1, STEPS)
    def _(t):
        @pl.loop(0, cols // GROUP)
        def _(g):
            base = g * GROUP
            args = (t, base, GROUP, SUB, span, near, here, lane)
            for i, (x, change) in enumerate(spread(xb, *args)):
                heat = yb[0, base + 1 + i, pl.ds(SUB, span)]
                w = xb[0, base + 1 + i, pl.ds(SUB, span)] - change
                xb[0, base + 1 + i, pl.ds(SUB, span)] = w
                xb[t + 1, base + 1 + i, pl.ds(SUB, span)] = (DAMPING + COUPLING * heat) * x + (heat - w)
            for i, (y, change) in enumerate(spread(yb, *args)):
                heat = yb[0, base + 1 + i, pl.ds(SUB, span)]
                w = wy[base + i] - change
                wy[base + i] = w
                yb[t + 1, base + 1 + i, pl.ds(SUB, span)] = (DAMPING + COUPLING * heat) * y - w

        pad_left(xb, t + 1)
        pad_left(yb, t + 1)

    def grad_copy(owner, slot):
        return pltpu.make_async_remote_copy(
            src_ref=part.at[pl.ds(owner * block, block)], dst_ref=share.at[me],
            send_sem=rs_send.at[slot], recv_sem=rs_recv.at[me],
            device_id={"path": owner}, device_id_type=MESH)

    def gradient(owner):
        @pl.loop(0, block)
        def _(i):
            j = owner * block + i
            both = [yb[1 + t, 1 + j, pl.ds(TOP, rows + SUB)] for t in range(STEPS)]
            add = both[0]
            for t in range(1, STEPS):
                add = add + both[t]
            mix = both[STEPS - 1][:rows] * xb[1, 1 + j, pl.ds(TOP, rows)]
            for t in range(1, STEPS):
                mix = mix + both[STEPS - 1 - t][:rows] * xb[1 + t, 1 + j, pl.ds(TOP, rows)]
            total[j] = add
            part[j] = beam[j] * (HEATING * add[:rows] + (HEATING * COUPLING) * mix)

    @pl.loop(1, n)
    def _(d):
        owner = lax.rem(me + d, n)
        gradient(owner)
        grad_copy(owner, d).start()

    gradient(me)

    inner = slice(SUB, SUB + rows)

    @pl.loop(0, cols // GROUP)
    def _(g):
        base = g * GROUP
        found = spread(yb, STEPS, base, GROUP, TOP, rows, near[inner], here[inner], lane[inner])
        for i, (y, change) in enumerate(found):
            j = base + i
            heat = yb[0, 1 + j, pl.ds(TOP, rows)]
            w = wy[j, pl.ds(SUB, rows)] - change
            final = (DAMPING + COUPLING * heat) * y - w
            add = total[j, pl.ds(0, rows)]
            across = KAPPA * (total[j, pl.ds(1, rows)] - add)
            after = jnp.where(lane_of == LANES - 1, pltpu.roll(total[j + 1, pl.ds(0, rows)], LANES - 1, 1),
                              pltpu.roll(add, LANES - 1, 1))
            along = KAPPA * (after - add)
            for r in range(row_tiles):
                cut = slice(r * SUB, r * SUB + SUB)
                done[0, r, j] = final[cut]
                done[1, r, j] = across[cut]
                done[2, r, j] = along[cut]

    out_a = pltpu.make_async_copy(done, out_state, out_sem.at[0])
    out_a.start()

    for i in range(block):
        for r in range(row_tiles):
            gsum[r, i] = part[me * block + i, pl.ds(r * SUB, SUB)]

    @pl.loop(1, n)
    def _(d):
        source = lax.rem(me + n - d, n)
        pltpu.make_async_remote_copy(
            src_ref=part.at[pl.ds(0, block)], dst_ref=share.at[source],
            send_sem=rs_send.at[d], recv_sem=rs_recv.at[source],
            device_id={"path": source}, device_id_type=MESH).wait_recv()
        for i in range(block):
            for r in range(row_tiles):
                gsum[r, i] = gsum[r, i] + share[source, i, pl.ds(r * SUB, SUB)]

    out_b = pltpu.make_async_copy(gsum, out_grad, out_sem.at[1])
    out_b.start()

    for copy in sends:
        copy.wait_send()

    @pl.loop(1, n)
    def _(d):
        grad_copy(lax.rem(me + d, n), d).wait_send()

    @pl.when(has_up)
    def _():
        state_copy(0).wait_send()

        @pl.loop(0, n)
        def _(b):
            heat_copy(0, b).wait_send()

    @pl.when(has_down)
    def _():
        state_copy(1).wait_send()

        @pl.loop(0, n)
        def _(b):
            heat_copy(1, b).wait_send()

    out_a.wait()
    out_b.wait()


def tiled(x):
    lead, (rows, cols) = x.shape[:-2], x.shape[-2:]
    return jnp.swapaxes(x.reshape(*lead, rows // SUB, SUB, cols // LANES, LANES), -3, -2)


def untiled(x):
    lead, (row_tiles, cols) = x.shape[:-4], x.shape[-4:-2]
    return jnp.swapaxes(x, -3, -2).reshape(*lead, row_tiles * SUB, cols * LANES)


def per_device(n, tiles, state0, intensity, absorption, screen_adjoint):
    rows, columns = intensity.shape[1:]
    cols, row_tiles = columns // LANES, rows // SUB
    block = cols // n
    height = rows + 4 * SUB
    f32 = jnp.float32
    dma = pltpu.SemaphoreType.DMA
    state_adjoint, grad = pl.pallas_call(
        functools.partial(kernel, n, tiles),
        out_shape=(
            jax.ShapeDtypeStruct((3, row_tiles, cols, SUB, LANES), f32),
            jax.ShapeDtypeStruct((row_tiles, block, SUB, LANES), f32),
        ),
        in_specs=[pl.BlockSpec(memory_space=pl.ANY)] * 4,
        out_specs=[pl.BlockSpec(memory_space=pl.ANY)] * 2,
        scratch_shapes=[
            pltpu.VMEM((STEPS + 1, cols + 2, height, LANES), f32),
            pltpu.VMEM((STEPS + 1, cols + 2, height, LANES), f32),
            pltpu.VMEM((cols, rows + 2 * SUB, LANES), f32),
            pltpu.VMEM((2, cols, rows, LANES), f32),
            pltpu.VMEM((cols, rows, LANES), f32),
            pltpu.VMEM((cols, rows, LANES), f32),
            pltpu.VMEM((cols + 1, rows, LANES), f32),
            pltpu.VMEM((2, 2, cols, SUB, LANES), f32),
            pltpu.VMEM((cols + 1, rows + SUB, LANES), f32),
            pltpu.VMEM((cols, rows, LANES), f32),
            pltpu.VMEM((n, block, rows, LANES), f32),
            pltpu.VMEM((3, row_tiles, cols, SUB, LANES), f32),
            pltpu.VMEM((row_tiles, block, SUB, LANES), f32),
            dma((6 * row_tiles,)),
            dma((2 * n,)),
            dma((n,)),
            dma((2,)),
            dma((2,)),
            dma((2, n)),
            dma((2, n)),
            dma((n,)),
            dma((n,)),
            dma((2,)),
        ],
        compiler_params=pltpu.CompilerParams(
            collective_id=0, has_side_effects=True, vmem_limit_bytes=60 * 1024 * 1024),
    )(tiled(state0[:, 0]), tiled(intensity[0]), tiled(absorption), tiled(screen_adjoint))
    return (untiled(state_adjoint)[:, None], untiled(grad))


def solution(mesh):
    return jax.shard_map(
        functools.partial(per_device, mesh.shape["path"], mesh.shape["tile"]),
        mesh=mesh,
        in_specs=(
            P(None, "path", "tile", None),
            P("path", "tile", None),
            P("tile", "path"),
            P("tile", "path"),
        ),
        out_specs=(P(None, "path", "tile", None), P("tile", "path")),
        check_vma=False,
    )
```

time: 280 us -> 39 us (0.14); the launches traced: 277 us -> 38.8 us
  starting transfers between devices: 110 us -> 0 us
  waiting for transfers between devices: 68.9 us -> 0 us
  blocking collectives: 51 us -> 0 us
  Pallas kernels: 0 us -> 35.5 us
  other arithmetic: 19.4 us -> 0 us
  between operations: 14.1 us -> 0.65 us
  local copies, waits for them, and re-layouts: 12 us -> 2.69 us
    ppermute x32 -> x0, starting transfers between devices: 110 us -> none  [the longest x16 66.4 us: padded(): before = lax.ppermute(last, axis, up)]
    reduce_scatter x1 -> x0, waiting for transfers between devices: 60.1 us -> none  [per_device(): lax.psum_scatter(local_grad, 'path', scatter_dimension=1, tiled=True)]
    all_gather x2 -> x0, blocking collectives: 51 us -> none  [the longest x1 26.1 us: per_device(): lax.all_gather(absorption, 'path', axis=1, tiled=True)]
    pallas_call x0 -> x1, Pallas kernels: none -> 35.5 us  [per_device(): pl.pallas_call(functools.partial(kernel, n, tiles), out_shape=(jax.ShapeD...]
    mul x49 -> x0, other arithmetic: 14.8 us -> none  [the longest x8 10.4 us: retreat(): ((DAMPING + HEATING * COUPLING * heat) * dual_density + KAPPA * (dual_acr...]
    ppermute x32 -> x0, waiting for transfers between devices: 8.75 us -> none  [the longest x16 8.71 us: padded(): before = lax.ppermute(last, axis, up)]
    dynamic_update_slice x8 -> x0, local copies, waits for them, and re-layouts: 5.9 us -> none  [per_device(): final_state, history = lax.scan(forward_one, start, None, length=STEPS)]
    slice x56 -> x0, local copies, waits for them, and re-layouts: 4.4 us -> none  [the longest x16 2.52 us: col_after(): return jnp.pad(field[:, :, 1:], ((0, 0), (0, 0), (0, 1)))]
  transfers between devices with their start and end apart: 33 -> 0, of which waited for: 17 -> 0; matrix products, arithmetic and copies ran while one was open for 3% -> 0% of each run, Pallas kernels for 0% -> 0%
where the time goes in v1:
time: 39 us; the launch traced here: 38.8 us
  Pallas kernels  35.5 us (91%)
  local copies, waits for them, and re-layouts  2.69 us (7%)
  between operations  0.65 us (2%)
    pallas_call x1, Pallas kernels, per_device(): pl.pallas_call(functools.partial(kernel, n, tiles), out_shape=(jax.ShapeD...  35.5 us
    unnamed x4, local copies, waits for them, and re-layouts  2.69 us

profile of v1, /device:TPU:1, one launch (start us, length us, event | category | flops | bytes accessed | tf_op | source)
XLA Modules:
  0.0 38.8 jit_solution(12534376240174654410)
XLA Ops:
  0.6 35.5 %shard_map.59 = (f32[3,2,32,8,128]{4,3,2,1,0:T(8,128)}, f32[2,4,8,128]{3,2,1,0:T(8,128)}) custom-call(f32[3,2,32,8,128]{4,3,2,1,0:T(8,128)} %bitcast.19, f32[2,32,8,128]{3,2,1,0:T(8,128)} %bitcast.20, f32[2,4,8,128]{3,2,1,0:T(8,128)} %bitcast.21, f32[2,4,8,128]{3,2,1,0:T(8,128)} %bitcast.22), custom_call_target="tpu_custom_call" | custom-call | tf_op jit(solution)/shard_map/pallas_call | solution.py:375
  36.1 0.0 copy-start
  36.1 2.1 %copy.8 = f32[3,1,16,4096]{3,2,1,0:T(8,128)} copy(f32[3,1,16,4096]{3,2,1,0:T(8,128)} %bitcast.18) | data formatting | bytes 1572864
  38.2 0.0 copy-done
  38.2 0.6 %copy.9 = f32[16,512]{1,0:T(8,128)} copy(f32[16,512]{1,0:T(8,128)S(1)} %bitcast.23) | data formatting | bytes 65536
Async XLA Ops:
  36.1 2.1 %copy-start = (f32[2,4,8,128]{3,2,1,0:T(8,128)S(1)}, f32[2,4,8,128]{3,2,1,0:T(8,128)}, u32[]{:S(2)}) copy-start(f32[2,4,8,128]{3,2,1,0:T(8,128)} %get-tuple-element.5) | copy-start | bytes 98308

commit v2 on v1

--- a/solution.py
+++ b/solution.py
@@ -17,7 +17,8 @@
 SUB = 8
 DEPTH = 4
 TOP = 2 * SUB
-GROUP = 4
+GROUP = 32
+UNROLL = 8
 
 
 def kernel(n, tiles, state, light, absorb, screen, out_state, out_grad,
@@ -29,6 +30,7 @@
     rows = row_tiles * SUB
     span = rows + 2 * SUB
     block = cols // n
+    group = GROUP if cols % GROUP == 0 else block
     me = lax.axis_index("path")
     tile = lax.axis_index("tile")
     my_z, my_y = me // wide, lax.rem(me, wide)
@@ -88,7 +90,7 @@
         xb[t, cols + 1, pl.ds(SUB, span)] = blank
         yb[t, cols + 1, pl.ds(SUB, span)] = blank
 
-    @pl.loop(0, cols)
+    @pl.loop(0, cols, unroll=UNROLL)
     def _(j):
         wy[j] = blank
 
@@ -96,14 +98,14 @@
 
     @pl.when(jnp.logical_not(has_up))
     def _():
-        @pl.loop(0, cols)
+        @pl.loop(0, cols, unroll=UNROLL)
         def _(j):
             xb[pl.ds(0, 2), 1 + j, pl.ds(SUB, SUB)] = strip
             yb[pl.ds(0, 2), 1 + j, pl.ds(SUB, SUB)] = strip
 
     @pl.when(jnp.logical_not(has_down))
     def _():
-        @pl.loop(0, cols)
+        @pl.loop(0, cols, unroll=UNROLL)
         def _(j):
             xb[pl.ds(0, 2), 1 + j, pl.ds(TOP + rows, SUB)] = strip
             yb[pl.ds(0, 2), 1 + j, pl.ds(TOP + rows, SUB)] = strip
@@ -114,7 +116,7 @@
     row_of = lax.broadcasted_iota(jnp.int32, (rows, LANES), 0)
     lane_of = lax.broadcasted_iota(jnp.int32, (rows, LANES), 1)
 
-    @pl.loop(0, cols)
+    @pl.loop(0, cols, unroll=UNROLL)
     def _(j):
         u, v = ub[j], vb[1 + j]
         before = jnp.where(row_of == 0, 0.0, pltpu.roll(u, 1, 0))
@@ -184,7 +186,7 @@
     def _():
         state_copy(1).wait_recv()
 
-        @pl.loop(0, cols)
+        @pl.loop(0, cols, unroll=UNROLL)
         def _(j):
             above = jnp.where(row_of[:SUB] == 0, xb[0, 1 + j, pl.ds(SUB, SUB)], 0.0)
             xb[0, 1 + j, pl.ds(TOP, SUB)] = xb[0, 1 + j, pl.ds(TOP, SUB)] - above
@@ -193,7 +195,7 @@
     def _():
         state_copy(0).wait_recv()
 
-        @pl.loop(0, cols)
+        @pl.loop(0, cols, unroll=UNROLL)
         def _(j):
             last = KAPPA * pltpu.roll(ub[j, pl.ds(rows - SUB, SUB)], 1, 0)
             above = jnp.where(row_of[:SUB] == 0, last, 0.0)
@@ -239,10 +241,10 @@
 
     @pl.loop(1, STEPS)
     def _(t):
-        @pl.loop(0, cols // GROUP)
+        @pl.loop(0, cols // group)
         def _(g):
-            base = g * GROUP
-            args = (t, base, GROUP, SUB, span, near, here, lane)
+            base = g * group
+            args = (t, base, group, SUB, span, near, here, lane)
             for i, (x, change) in enumerate(spread(xb, *args)):
                 heat = yb[0, base + 1 + i, pl.ds(SUB, span)]
                 w = xb[0, base + 1 + i, pl.ds(SUB, span)] - change
@@ -264,7 +266,7 @@
             device_id={"path": owner}, device_id_type=MESH)
 
     def gradient(owner):
-        @pl.loop(0, block)
+        @pl.loop(0, block, unroll=block)
         def _(i):
             j = owner * block + i
             both = [yb[1 + t, 1 + j, pl.ds(TOP, rows + SUB)] for t in range(STEPS)]
@@ -287,10 +289,10 @@
 
     inner = slice(SUB, SUB + rows)
 
-    @pl.loop(0, cols // GROUP)
+    @pl.loop(0, cols // group)
     def _(g):
-        base = g * GROUP
-        found = spread(yb, STEPS, base, GROUP, TOP, rows, near[inner], here[inner], lane[inner])
+        base = g * group
+        found = spread(yb, STEPS, base, group, TOP, rows, near[inner], here[inner], lane[inner])
         for i, (y, change) in enumerate(found):
             j = base + i
             heat = yb[0, 1 + j, pl.ds(TOP, rows)]
@@ -355,6 +357,19 @@
     out_b.wait()
 
 
+def settle(state, grad, out_state, out_grad, state_held, grad_held, sem):
+    pairs = [(state.at[c], state_held.at[c], out_state.at[c]) for c in range(3)] + [(grad, grad_held, out_grad)]
+    gets = [pltpu.make_async_copy(x, y, sem.at[0, i]) for i, (x, y, z) in enumerate(pairs)]
+    puts = [pltpu.make_async_copy(y, z, sem.at[1, i]) for i, (x, y, z) in enumerate(pairs)]
+    for get in gets:
+        get.start()
+    for get, put in zip(gets, puts):
+        get.wait()
+        put.start()
+    for put in puts:
+        put.wait()
+
+
 def tiled(x):
     lead, (rows, cols) = x.shape[:-2], x.shape[-2:]
     return jnp.swapaxes(x.reshape(*lead, rows // SUB, SUB, cols // LANES, LANES), -3, -2)
@@ -372,14 +387,16 @@
     height = rows + 4 * SUB
     f32 = jnp.float32
     dma = pltpu.SemaphoreType.DMA
-    state_adjoint, grad = pl.pallas_call(
+    shapes = (
+        jax.ShapeDtypeStruct((3, row_tiles, cols, SUB, LANES), f32),
+        jax.ShapeDtypeStruct((row_tiles, block, SUB, LANES), f32),
+    )
+    whole = pl.BlockSpec(memory_space=pl.ANY)
+    found = pl.pallas_call(
         functools.partial(kernel, n, tiles),
-        out_shape=(
-            jax.ShapeDtypeStruct((3, row_tiles, cols, SUB, LANES), f32),
-            jax.ShapeDtypeStruct((row_tiles, block, SUB, LANES), f32),
-        ),
-        in_specs=[pl.BlockSpec(memory_space=pl.ANY)] * 4,
-        out_specs=[pl.BlockSpec(memory_space=pl.ANY)] * 2,
+        out_shape=shapes,
+        in_specs=[whole] * 4,
+        out_specs=[whole] * 2,
         scratch_shapes=[
             pltpu.VMEM((STEPS + 1, cols + 2, height, LANES), f32),
             pltpu.VMEM((STEPS + 1, cols + 2, height, LANES), f32),
@@ -408,6 +425,14 @@
         compiler_params=pltpu.CompilerParams(
             collective_id=0, has_side_effects=True, vmem_limit_bytes=60 * 1024 * 1024),
     )(tiled(state0[:, 0]), tiled(intensity[0]), tiled(absorption), tiled(screen_adjoint))
+    state_adjoint, grad = pl.pallas_call(
+        settle,
+        out_shape=shapes,
+        in_specs=[whole] * 2,
+        out_specs=[whole] * 2,
+        scratch_shapes=[pltpu.VMEM(x.shape, f32) for x in shapes] + [dma((2, 4))],
+        compiler_params=pltpu.CompilerParams(vmem_limit_bytes=60 * 1024 * 1024),
+    )(*found)
     return (untiled(state_adjoint)[:, None], untiled(grad))
 
 

time: 39 us -> 34.5 us (0.88)
  local copies, waits for them, and re-layouts: 2.69 us -> 0 us
  Pallas kernels: 35.5 us -> 33.7 us
    unnamed x4 -> x0, local copies, waits for them, and re-layouts: 2.69 us -> none
    pallas_call x1 -> x2, Pallas kernels: 35.5 us -> 33.7 us  [the longest x1 31.8 us: per_device(): pl.pallas_call(functools.partial(kernel, n, tiles), out_shape=shapes, in_...]
where the time goes in v2:
time: 34.5 us; the launch traced here: 34.4 us
  Pallas kernels  33.7 us (98%)
  between operations  0.64 us (2%)
    pallas_call x1, Pallas kernels, per_device(): pl.pallas_call(functools.partial(kernel, n, tiles), out_shape=shapes, in_...  31.8 us
    pallas_call x1, Pallas kernels, per_device(): pl.pallas_call(settle, out_shape=shapes, in_specs=[whole] * 2, out_specs=...  1.9 us

profile of v2, /device:TPU:1, one launch (start us, length us, event | category | flops | bytes accessed | tf_op | source)
XLA Modules:
  0.0 34.4 jit_solution(15144901156293370132)
XLA Ops:
  0.6 31.8 %shard_map.59 = (f32[3,2,32,8,128]{4,3,2,1,0:T(8,128)}, f32[2,4,8,128]{3,2,1,0:T(8,128)}) custom-call(f32[3,2,32,8,128]{4,3,2,1,0:T(8,128)} %bitcast.18, f32[2,32,8,128]{3,2,1,0:T(8,128)} %bitcast.19, f32[2,4,8,128]{3,2,1,0:T(8,128)} %bitcast.20, f32[2,4,8,128]{3,2,1,0:T(8,128)} %bitcast.21), custom_call_target="tpu_custom_call" | custom-call | tf_op jit(solution)/shard_map/pallas_call | solution.py:395
  32.5 1.9 %shard_map.60 = (f32[3,2,32,8,128]{4,3,2,1,0:T(8,128)}, f32[2,4,8,128]{3,2,1,0:T(8,128)}) custom-call(f32[3,2,32,8,128]{4,3,2,1,0:T(8,128)} %get-tuple-element.6.state, f32[2,4,8,128]{3,2,1,0:T(8,128)} %get-tuple-element.7.grad), custom_call_target="tpu_custom_call" | custom-call | tf_op jit(solution)/shard_map/pallas_call | solution.py:428

commit v3 on v2

--- a/solution.py
+++ b/solution.py
@@ -76,7 +76,7 @@
         loads[6 * i].wait()
         loads[6 * i + 1].wait()
     sends = []
-    for d in [x for x in (2, 1, 3) if x < depth]:
+    for d in [x for x in (1, 3, 2) if x < depth]:
         sends.append(map_copy(me, lax.rem(my_z + d, depth) * wide + my_y, len(sends)))
         sends[-1].start()
     for d in range(1, wide):

time: 34.5 us -> 33 us (0.957)
  Pallas kernels: 33.7 us -> 32.2 us
    pallas_call x1, Pallas kernels: 31.8 us -> 30.4 us  [per_device(): pl.pallas_call(functools.partial(kernel, n, tiles), out_shape=shapes, in_...]
where the time goes in v3:
time: 33 us; the launch traced here: 32.9 us
  Pallas kernels  32.2 us (98%)
  between operations  0.64 us (2%)
    pallas_call x1, Pallas kernels, per_device(): pl.pallas_call(functools.partial(kernel, n, tiles), out_shape=shapes, in_...  30.4 us
    pallas_call x1, Pallas kernels, per_device(): pl.pallas_call(settle, out_shape=shapes, in_specs=[whole] * 2, out_specs=...  1.9 us

profile of v3, /device:TPU:1, one launch (start us, length us, event | category | flops | bytes accessed | tf_op | source)
XLA Modules:
  0.0 32.9 jit_solution(3398337544919064138)
XLA Ops:
  0.6 30.4 %shard_map.59 = (f32[3,2,32,8,128]{4,3,2,1,0:T(8,128)}, f32[2,4,8,128]{3,2,1,0:T(8,128)}) custom-call(f32[3,2,32,8,128]{4,3,2,1,0:T(8,128)} %bitcast.18, f32[2,32,8,128]{3,2,1,0:T(8,128)} %bitcast.19, f32[2,4,8,128]{3,2,1,0:T(8,128)} %bitcast.20, f32[2,4,8,128]{3,2,1,0:T(8,128)} %bitcast.21), custom_call_target="tpu_custom_call" | custom-call | tf_op jit(solution)/shard_map/pallas_call | solution.py:395
  31.0 1.9 %shard_map.60 = (f32[3,2,32,8,128]{4,3,2,1,0:T(8,128)}, f32[2,4,8,128]{3,2,1,0:T(8,128)}) custom-call(f32[3,2,32,8,128]{4,3,2,1,0:T(8,128)} %get-tuple-element.6.state, f32[2,4,8,128]{3,2,1,0:T(8,128)} %get-tuple-element.7.grad), custom_call_target="tpu_custom_call" | custom-call | tf_op jit(solution)/shard_map/pallas_call | solution.py:428
